TPU v7x, 32 devices: a whole 2x2x4 slice. The times are simulated.
32 devices in a mesh: groups: 2 (over y), dap: 4 (over z), dp: 4 (over x, core).
Axes of the slice: x: 2, y: 2, z: 4, core: 2. Of those that a mesh axis runs over, the one named last changes fastest.
Arguments:
- pair: bfloat16 [8, 128, 16, 16], P(('groups', 'dp'), None, 'dap'), parts along dimension 0, may hold values from -6 to 6
- cotangent: bfloat16 [8, 128, 16, 16], P(('groups', 'dp'), None, 'dap'), parts along dimension 0, may hold values from -6 to 6
- proj_weight: bfloat16 [2, 512, 128], replicated, may hold values from -0.5 to 0.5
- proj_bias: float32 [2, 512], replicated, may hold values from -3 to 3
- gate_weight: bfloat16 [2, 128, 128], replicated, may hold values from -0.5 to 0.5
- out_weight: bfloat16 [2, 128, 128], replicated, may hold values from -0.5 to 0.5
- chan_bias: float32 [2, 2, 128], replicated, may hold values from -3 to 3
- norm_gain: float32 [2, 2, 128], replicated, may hold values from 0.25 to 1.75
- norm_shift: float32 [2, 2, 128], replicated, may hold values from -3 to 3
Outputs:
- grad_pair: bfloat16 [8, 128, 16, 16], P(('groups', 'dp'), None, 'dap'), parts along dimension 0
- grad_proj_weight: float32 [4, 512, 128], P('groups'), parts along dimension 0
- grad_proj_bias: float32 [4, 512], P('groups'), parts along dimension 0
- grad_gate_weight: float32 [4, 128, 128], P('groups'), parts along dimension 0
- grad_out_weight: float32 [4, 128, 128], P('groups'), parts along dimension 0
- grad_chan_bias: float32 [4, 2, 128], P('groups'), parts along dimension 0
- grad_norm_gain: float32 [4, 2, 128], P('groups'), parts along dimension 0
- grad_norm_shift: float32 [4, 2, 128], P('groups'), parts along dimension 0
There are 2 independent parts, one for each index of `groups`. A program takes and returns all parts, laid end to end along the dimension named above; an argument that names none is the same for every part. Nothing has to cross between parts.
All inputs are finite; a program needn't handle non-finite values.
Results may differ from a plain program's by a relative error of at most 0.01.
Values may be sent and summed in bfloat16 or wider, within the bound.
A program may use at most 64 MiB of HBM per device.

v0:
```python
import jax
import jax.numpy as jnp
from jax import lax
from jax.sharding import PartitionSpec as P

EPSILON = 1e-05


def normalize(values, scale_by, offset):
    average = jnp.mean(values, axis=0, keepdims=True)
    centred = values - average
    variance = jnp.mean(centred * centred, axis=0, keepdims=True)
    inverse = lax.rsqrt(variance + EPSILON)
    standard = centred * inverse
    return (standard * scale_by[:, None] + offset[:, None], standard, inverse)


def normalize_back(upstream, scale_by, standard, inverse):
    scaled = upstream * scale_by[:, None]
    adjusted = (
        scaled
        - jnp.mean(scaled, axis=0, keepdims=True)
        - standard * jnp.mean(scaled * standard, axis=0, keepdims=True)
    )
    return (inverse * adjusted, jnp.sum(upstream * standard, axis=1), jnp.sum(upstream, axis=1))


def matmul_rows(left, right):
    return lax.dot_general(
        left, right, (((1,), (1,)), ((), ())), preferred_element_type=jnp.float32
    )


def matmul_cols(left, right):
    return lax.dot_general(
        left, right, (((0,), (0,)), ((), ())), preferred_element_type=jnp.float32
    )


def contract(left, right, left_dim, right_dim):
    return lax.dot_general(
        left, right, (((left_dim,), (right_dim,)), ((0,), (0,))), preferred_element_type=jnp.float32
    )


def forward_update(pair_rows, params, layer, dims, incoming):
    proj_weight, proj_bias, gate_weight, out_weight, chan_bias, norm_gain, norm_shift = params
    channels, rows, width = dims
    source = pair_rows.astype(jnp.float32)
    normed, standard_in, inverse_in = normalize(source, norm_gain[layer, 0], norm_shift[layer, 0])
    inputs = normed.astype(jnp.bfloat16)
    weight_now = proj_weight[layer]
    bias_now = proj_bias[layer]

    def gated(first_row):
        pre_act = jnp.dot(
            weight_now[first_row : first_row + 2 * channels],
            inputs,
            preferred_element_type=jnp.float32,
        )
        pre_act = pre_act + bias_now[first_row : first_row + 2 * channels][:, None]
        value = pre_act[:channels]
        logit = pre_act[channels:]
        product = (
            (jax.nn.sigmoid(logit) * value).astype(jnp.bfloat16).reshape(channels, rows, width)
        )
        return (product, value, logit)

    left_rows, left_value, left_logit = gated(0)
    left_cols = lax.all_to_all(left_rows, "dap", split_axis=0, concat_axis=1, tiled=True)
    right_rows, right_value, right_logit = gated(2 * channels)
    right_cols = lax.all_to_all(right_rows, "dap", split_axis=0, concat_axis=1, tiled=True)
    gate = jax.nn.sigmoid(
        jnp.dot(gate_weight[layer], inputs, preferred_element_type=jnp.float32)
        + chan_bias[layer, 0][:, None]
    )
    if incoming:
        triangle = contract(left_cols, right_cols, 1, 1)
    else:
        triangle = contract(left_cols, right_cols, 2, 2)
    triangle_rows = lax.all_to_all(
        triangle.astype(jnp.bfloat16), "dap", split_axis=1, concat_axis=0, tiled=True
    )
    triangle_rows = triangle_rows.reshape(channels, rows * width)
    normed_tri, standard_out, inverse_out = normalize(
        triangle_rows.astype(jnp.float32), norm_gain[layer, 1], norm_shift[layer, 1]
    )
    tri_inputs = normed_tri.astype(jnp.bfloat16)
    linear = (
        jnp.dot(out_weight[layer], tri_inputs, preferred_element_type=jnp.float32)
        + chan_bias[layer, 1][:, None]
    )
    next_pair = (source + gate * linear).astype(jnp.bfloat16)
    saved = (
        inputs,
        standard_in,
        inverse_in,
        left_value,
        left_logit,
        right_value,
        right_logit,
        left_cols,
        right_cols,
        gate,
        linear,
        tri_inputs,
        standard_out,
        inverse_out,
    )
    return (next_pair, saved)


def backward_update(upstream, saved, params, layer, dims, incoming):
    proj_weight, proj_bias, gate_weight, out_weight, chan_bias, norm_gain, norm_shift = params
    channels, rows, width = dims
    (
        inputs,
        standard_in,
        inverse_in,
        left_value,
        left_logit,
        right_value,
        right_logit,
        left_cols,
        right_cols,
        gate,
        linear,
        tri_inputs,
        standard_out,
        inverse_out,
    ) = saved
    grad_linear = (upstream * gate).astype(jnp.bfloat16)
    grad_logit = (upstream * linear * gate * (1.0 - gate)).astype(jnp.bfloat16)
    grad_out_w = matmul_rows(grad_linear, tri_inputs)
    grad_out_b = jnp.sum(grad_linear.astype(jnp.float32), axis=1)
    grad_gate_w = matmul_rows(grad_logit, inputs)
    grad_gate_b = jnp.sum(grad_logit.astype(jnp.float32), axis=1)
    grad_normed = matmul_cols(out_weight[layer], grad_linear)
    grad_tri, gain_out, shift_out = normalize_back(
        grad_normed, norm_gain[layer, 1], standard_out, inverse_out
    )
    grad_cols = lax.all_to_all(
        grad_tri.astype(jnp.bfloat16).reshape(channels, rows, width),
        "dap",
        split_axis=0,
        concat_axis=1,
        tiled=True,
    )

    def left_term():
        if incoming:
            return contract(right_cols, grad_cols, 2, 2).astype(jnp.bfloat16)
        return contract(grad_cols, right_cols, 2, 1).astype(jnp.bfloat16)

    def right_term():
        if incoming:
            return contract(left_cols, grad_cols, 2, 1).astype(jnp.bfloat16)
        return contract(grad_cols, left_cols, 1, 1).astype(jnp.bfloat16)

    left_back = lax.all_to_all(left_term(), "dap", split_axis=1, concat_axis=0, tiled=True)
    right_back = lax.all_to_all(right_term(), "dap", split_axis=1, concat_axis=0, tiled=True)
    left_back = left_back.reshape(channels, rows * width).astype(jnp.float32)
    right_back = right_back.reshape(channels, rows * width).astype(jnp.float32)
    left_sig = jax.nn.sigmoid(left_logit)
    right_sig = jax.nn.sigmoid(right_logit)
    grad_pre = jnp.concatenate(
        [
            left_back * left_sig,
            left_back * left_value * left_sig * (1.0 - left_sig),
            right_back * right_sig,
            right_back * right_value * right_sig * (1.0 - right_sig),
        ],
        axis=0,
    ).astype(jnp.bfloat16)
    grad_proj_w = matmul_rows(grad_pre, inputs)
    grad_proj_b = jnp.sum(grad_pre.astype(jnp.float32), axis=1)
    grad_inputs = matmul_cols(proj_weight[layer], grad_pre) + matmul_cols(
        gate_weight[layer], grad_logit
    )
    grad_source, gain_in, shift_in = normalize_back(
        grad_inputs, norm_gain[layer, 0], standard_in, inverse_in
    )
    grads = (
        grad_proj_w,
        grad_proj_b,
        grad_gate_w,
        grad_out_w,
        jnp.stack([grad_gate_b, grad_out_b]),
        jnp.stack([gain_in, gain_out]),
        jnp.stack([shift_in, shift_out]),
    )
    return (upstream + grad_source, grads)


def body(
    pair,
    cotangent,
    proj_weight,
    proj_bias,
    gate_weight,
    out_weight,
    chan_bias,
    norm_gain,
    norm_shift,
):
    params = (proj_weight, proj_bias, gate_weight, out_weight, chan_bias, norm_gain, norm_shift)
    channels = pair.shape[1]
    rows = pair.shape[2]
    width = pair.shape[3]
    dims = (channels, rows, width)
    start_pair = pair[0].reshape(channels, rows * width)
    middle, saved_first = forward_update(start_pair, params, 0, dims, False)
    unused, saved_second = forward_update(middle, params, 1, dims, True)
    upstream = cotangent[0].reshape(channels, rows * width).astype(jnp.float32)
    grad_middle, grads_second = backward_update(upstream, saved_second, params, 1, dims, True)
    repeat_pair, saved_first = forward_update(start_pair, params, 0, dims, False)
    grad_start, grads_first = backward_update(grad_middle, saved_first, params, 0, dims, False)
    joined = tuple(
        (
            jnp.stack([first_part, second_part])
            for first_part, second_part in zip(grads_first, grads_second)
        )
    )
    stacked = lax.psum(
        (joined[0], joined[1], joined[2], joined[3], joined[4], joined[5], joined[6]), ("dap", "dp")
    )
    factor = 1.0 / width
    return (
        grad_start.astype(jnp.bfloat16).reshape(1, channels, rows, width),
        stacked[0] * factor,
        stacked[1] * factor,
        stacked[2] * factor,
        stacked[3] * factor,
        stacked[4] * factor,
        stacked[5] * factor,
        stacked[6] * factor,
    )


def solution(mesh):
    in_specs = (
        P(("groups", "dp"), None, "dap", None),
        P(("groups", "dp"), None, "dap", None),
        P(),
        P(),
        P(),
        P(),
        P(),
        P(),
        P(),
    )
    out_specs = (
        P(("groups", "dp"), None, "dap", None),
        P("groups", None, None),
        P("groups", None),
        P("groups", None, None),
        P("groups", None, None),
        P("groups", None, None),
        P("groups", None, None),
        P("groups", None, None),
    )
    return jax.shard_map(body, mesh=mesh, in_specs=in_specs, out_specs=out_specs, check_vma=False)
```

profile of v0, /device:TPU:0, one launch (start us, length us, event | category | flops | bytes accessed | tf_op | source)
XLA Modules:
  0.0 299.7 jit_solution(5875431716307852703)
XLA Ops:
  7.2 0.9 convert_reduce_fusion.3
  8.2 0.7 copy-done.6
  8.9 0.7 copy-done.7
  9.7 1.0 fusion.3
  11.0 0.8 reshape.421
  11.7 6.3 %all-to-all-start = ((bf16[4,2,1024]{2,1,0:T(2,128)(2,1)}), bf16[4,2,1024]{2,1,0:T(2,128)(2,1)S(1)}, u32[]{:S(2)}, u32[]{:S(2)}) async-start(bf16[4,2,1024]{2,1,0:T(2,128)(2,1)} %reshape.421), calls=%async_computation | async-start | bytes 32768 | tf_op jit(solution)/shard_map/all_to_all | solution.py:70
  18.4 0.8 reshape.423
  19.1 4.5 %all-to-all-done = bf16[4,2,1024]{2,1,0:T(2,128)(2,1)S(1)} async-done(((bf16[4,2,1024]{2,1,0:T(2,128)(2,1)}), bf16[4,2,1024]{2,1,0:T(2,128)(2,1)S(1)}, u32[]{:S(2)}, u32[]{:S(2)}) %all-to-all-start) | async-done | bytes 16416 | tf_op jit(solution)/shard_map/all_to_all | solution.py:70
  23.7 3.3 %all-to-all-start.1 = ((bf16[4,2,1024]{2,1,0:T(2,128)(2,1)}), bf16[4,2,1024]{2,1,0:T(2,128)(2,1)S(1)}, u32[]{:S(2)}, u32[]{:S(2)}) async-start(bf16[4,2,1024]{2,1,0:T(2,128)(2,1)} %reshape.423), calls=%async_computation.1 | async-start | bytes 32768 | tf_op jit(solution)/shard_map/all_to_all | solution.py:72
  27.1 5.4 %all-to-all-done.1 = bf16[4,2,1024]{2,1,0:T(2,128)(2,1)S(1)} async-done(((bf16[4,2,1024]{2,1,0:T(2,128)(2,1)}), bf16[4,2,1024]{2,1,0:T(2,128)(2,1)S(1)}, u32[]{:S(2)}, u32[]{:S(2)}) %all-to-all-start.1) | async-done | bytes 16416 | tf_op jit(solution)/shard_map/all_to_all | solution.py:72
  33.1 0.7 reshape.425
  33.8 3.4 %all-to-all-start.2 = ((bf16[4,2,1024]{2,1,0:T(2,128)(2,1)}), bf16[4,2,1024]{2,1,0:T(2,128)(2,1)S(1)}, u32[]{:S(2)}, u32[]{:S(2)}) async-start(bf16[4,2,1024]{2,1,0:T(2,128)(2,1)} %reshape.425), calls=%async_computation.2 | async-start | bytes 32768 | tf_op jit(solution)/shard_map/all_to_all | solution.py:81
  37.4 5.4 %all-to-all-done.2 = bf16[4,2,1024]{2,1,0:T(2,128)(2,1)S(1)} async-done(((bf16[4,2,1024]{2,1,0:T(2,128)(2,1)}), bf16[4,2,1024]{2,1,0:T(2,128)(2,1)S(1)}, u32[]{:S(2)}, u32[]{:S(2)}) %all-to-all-start.2) | async-done | bytes 16416 | tf_op jit(solution)/shard_map/all_to_all | solution.py:81
  42.9 0.3 fusion.111
  43.2 0.5 multiply_reduce_fusion.1
  44.0 0.7 copy-done.5
  44.8 0.3 convert_reduce_fusion.2
  45.9 0.8 reshape.429
  46.7 3.3 %all-to-all-start.3 = ((bf16[4,2,1024]{2,1,0:T(2,128)(2,1)}), bf16[4,2,1024]{2,1,0:T(2,128)(2,1)S(1)}, u32[]{:S(2)}, u32[]{:S(2)}) async-start(bf16[4,2,1024]{2,1,0:T(2,128)(2,1)} %reshape.429), calls=%async_computation.3 | async-start | bytes 32768 | tf_op jit(solution)/shard_map/all_to_all | solution.py:72
  50.1 0.8 reshape.427
  50.9 4.6 %all-to-all-done.3 = bf16[4,2,1024]{2,1,0:T(2,128)(2,1)S(1)} async-done(((bf16[4,2,1024]{2,1,0:T(2,128)(2,1)}), bf16[4,2,1024]{2,1,0:T(2,128)(2,1)S(1)}, u32[]{:S(2)}, u32[]{:S(2)}) %all-to-all-start.3) | async-done | bytes 16416 | tf_op jit(solution)/shard_map/all_to_all | solution.py:72
  55.6 3.3 %all-to-all-start.4 = ((bf16[4,2,1024]{2,1,0:T(2,128)(2,1)}), bf16[4,2,1024]{2,1,0:T(2,128)(2,1)S(1)}, u32[]{:S(2)}, u32[]{:S(2)}) async-start(bf16[4,2,1024]{2,1,0:T(2,128)(2,1)} %reshape.427), calls=%async_computation.4 | async-start | bytes 32768 | tf_op jit(solution)/shard_map/all_to_all | solution.py:70
  59.4 5.0 %all-to-all-done.4 = bf16[4,2,1024]{2,1,0:T(2,128)(2,1)S(1)} async-done(((bf16[4,2,1024]{2,1,0:T(2,128)(2,1)}), bf16[4,2,1024]{2,1,0:T(2,128)(2,1)S(1)}, u32[]{:S(2)}, u32[]{:S(2)}) %all-to-all-start.4) | async-done | bytes 16416 | tf_op jit(solution)/shard_map/all_to_all | solution.py:70
  65.3 0.7 reshape.431
  66.0 3.4 %all-to-all-start.5 = ((bf16[4,2,1024]{2,1,0:T(2,128)(2,1)}), bf16[4,2,1024]{2,1,0:T(2,128)(2,1)S(1)}, u32[]{:S(2)}, u32[]{:S(2)}) async-start(bf16[4,2,1024]{2,1,0:T(2,128)(2,1)} %reshape.431), calls=%async_computation.5 | async-start | bytes 32768 | tf_op jit(solution)/shard_map/all_to_all | solution.py:81
  70.0 5.0 %all-to-all-done.5 = bf16[4,2,1024]{2,1,0:T(2,128)(2,1)S(1)} async-done(((bf16[4,2,1024]{2,1,0:T(2,128)(2,1)}), bf16[4,2,1024]{2,1,0:T(2,128)(2,1)S(1)}, u32[]{:S(2)}, u32[]{:S(2)}) %all-to-all-start.5) | async-done | bytes 16416 | tf_op jit(solution)/shard_map/all_to_all | solution.py:81
  75.1 0.3 fusion.112
  75.4 0.5 multiply_reduce_fusion
  77.7 0.8 reshape.433
  78.4 3.3 %all-to-all-start.6 = ((bf16[4,2,1024]{2,1,0:T(2,128)(2,1)}), bf16[4,2,1024]{2,1,0:T(2,128)(2,1)S(1)}, u32[]{:S(2)}, u32[]{:S(2)}) async-start(bf16[4,2,1024]{2,1,0:T(2,128)(2,1)} %reshape.433), calls=%async_computation.6 | async-start | bytes 32768 | tf_op jit(solution)/shard_map/all_to_all | solution.py:142
  81.7 5.5 %all-to-all-done.6 = bf16[4,2,1024]{2,1,0:T(2,128)(2,1)S(1)} async-done(((bf16[4,2,1024]{2,1,0:T(2,128)(2,1)}), bf16[4,2,1024]{2,1,0:T(2,128)(2,1)S(1)}, u32[]{:S(2)}, u32[]{:S(2)}) %all-to-all-start.6) | async-done | bytes 16416 | tf_op jit(solution)/shard_map/all_to_all | solution.py:142
  87.8 0.7 reshape.437
  88.6 3.3 %all-to-all-start.7 = ((bf16[4,2,1024]{2,1,0:T(2,128)(2,1)}), bf16[4,2,1024]{2,1,0:T(2,128)(2,1)S(1)}, u32[]{:S(2)}, u32[]{:S(2)}) async-start(bf16[4,2,1024]{2,1,0:T(2,128)(2,1)} %reshape.437), calls=%async_computation.7 | async-start | bytes 32768 | tf_op jit(solution)/shard_map/all_to_all | solution.py:160
  92.2 0.7 reshape.435
  92.9 4.5 %all-to-all-done.7 = bf16[4,2,1024]{2,1,0:T(2,128)(2,1)S(1)} async-done(((bf16[4,2,1024]{2,1,0:T(2,128)(2,1)}), bf16[4,2,1024]{2,1,0:T(2,128)(2,1)S(1)}, u32[]{:S(2)}, u32[]{:S(2)}) %all-to-all-start.7) | async-done | bytes 16416 | tf_op jit(solution)/shard_map/all_to_all | solution.py:160
  97.4 3.3 %all-to-all-start.8 = ((bf16[4,2,1024]{2,1,0:T(2,128)(2,1)}), bf16[4,2,1024]{2,1,0:T(2,128)(2,1)S(1)}, u32[]{:S(2)}, u32[]{:S(2)}) async-start(bf16[4,2,1024]{2,1,0:T(2,128)(2,1)} %reshape.435), calls=%async_computation.8 | async-start | bytes 32768 | tf_op jit(solution)/shard_map/all_to_all | solution.py:161
  101.0 5.3 %all-to-all-done.8 = bf16[4,2,1024]{2,1,0:T(2,128)(2,1)S(1)} async-done(((bf16[4,2,1024]{2,1,0:T(2,128)(2,1)}), bf16[4,2,1024]{2,1,0:T(2,128)(2,1)S(1)}, u32[]{:S(2)}, u32[]{:S(2)}) %all-to-all-start.8) | async-done | bytes 16416 | tf_op jit(solution)/shard_map/all_to_all | solution.py:161
  106.7 0.3 convolution_bitcast_fusion
  107.0 0.2 fusion.45
  107.4 0.2 fusion.61
  108.2 0.8 reshape.439
  108.9 3.3 %all-to-all-start.9 = ((bf16[4,2,1024]{2,1,0:T(2,128)(2,1)}), bf16[4,2,1024]{2,1,0:T(2,128)(2,1)S(1)}, u32[]{:S(2)}, u32[]{:S(2)}) async-start(bf16[4,2,1024]{2,1,0:T(2,128)(2,1)} %reshape.439), calls=%async_computation.9 | async-start | bytes 32768 | tf_op jit(solution)/shard_map/all_to_all | solution.py:142
  112.2 0.7 pad_maximum_fusion.2
  113.0 4.8 %all-to-all-done.9 = bf16[4,2,1024]{2,1,0:T(2,128)(2,1)S(1)} async-done(((bf16[4,2,1024]{2,1,0:T(2,128)(2,1)}), bf16[4,2,1024]{2,1,0:T(2,128)(2,1)S(1)}, u32[]{:S(2)}, u32[]{:S(2)}) %all-to-all-start.9) | async-done | bytes 16416 | tf_op jit(solution)/shard_map/all_to_all | solution.py:142
  118.3 0.7 reshape.443
  119.1 3.3 %all-to-all-start.10 = ((bf16[4,2,1024]{2,1,0:T(2,128)(2,1)}), bf16[4,2,1024]{2,1,0:T(2,128)(2,1)S(1)}, u32[]{:S(2)}, u32[]{:S(2)}) async-start(bf16[4,2,1024]{2,1,0:T(2,128)(2,1)} %reshape.443), calls=%async_computation.10 | async-start | bytes 32768 | tf_op jit(solution)/shard_map/all_to_all | solution.py:160
  122.7 0.7 reshape.441
  123.5 4.4 %all-to-all-done.10 = bf16[4,2,1024]{2,1,0:T(2,128)(2,1)S(1)} async-done(((bf16[4,2,1024]{2,1,0:T(2,128)(2,1)}), bf16[4,2,1024]{2,1,0:T(2,128)(2,1)S(1)}, u32[]{:S(2)}, u32[]{:S(2)}) %all-to-all-start.10) | async-done | bytes 16416 | tf_op jit(solution)/shard_map/all_to_all | solution.py:160
  127.9 3.3 %all-to-all-start.11 = ((bf16[4,2,1024]{2,1,0:T(2,128)(2,1)}), bf16[4,2,1024]{2,1,0:T(2,128)(2,1)S(1)}, u32[]{:S(2)}, u32[]{:S(2)}) async-start(bf16[4,2,1024]{2,1,0:T(2,128)(2,1)} %reshape.441), calls=%async_computation.11 | async-start | bytes 32768 | tf_op jit(solution)/shard_map/all_to_all | solution.py:161
  131.6 5.2 %all-to-all-done.11 = bf16[4,2,1024]{2,1,0:T(2,128)(2,1)S(1)} async-done(((bf16[4,2,1024]{2,1,0:T(2,128)(2,1)}), bf16[4,2,1024]{2,1,0:T(2,128)(2,1)S(1)}, u32[]{:S(2)}, u32[]{:S(2)}) %all-to-all-start.11) | async-done | bytes 16416 | tf_op jit(solution)/shard_map/all_to_all | solution.py:161
  137.3 0.3 fusion.60
  138.0 57.6 %all-reduce = (f32[2,512]{1,0:T(2,128)S(1)}, f32[2,2,128]{2,1,0:T(2,128)S(1)}, f32[2,2,128]{2,1,0:T(2,128)S(1)}, f32[2,2,128]{2,1,0:T(2,128)S(1)}) all-reduce(f32[2,512]{1,0:T(2,128)S(1)} %pad_maximum_fusion.5, f32[2,2,128]{2,1,0:T(2,128)S(1)} %pad_maximum_fusion.6, ...), channel_id=1, replica_groups=mesh['groups'=2,'dap'=4,'dp'=4] {'dap','dp'}, use_global_device_ids=true, to_apply=%region_19.0 | all-reduce | flops 2560 | bytes 20480 | tf_op jit(solution)/shard_map/psum | solution.py:224
  195.7 0.6 broadcast_multiply_fusion.3
  196.3 0.6 broadcast_multiply_fusion.6
  196.8 0.6 broadcast_multiply_fusion.5
  197.4 0.6 broadcast_multiply_fusion.4
  198.0 0.7 pad_maximum_fusion.1
  198.7 0.8 pad_maximum_fusion
  199.5 0.7 fusion.88
  200.3 89.1 %all-reduce.4.cloned.1.call-done = (f32[2,512,128]{2,1,0:T(8,128)}, f32[2,128,128]{2,1,0:T(8,128)}, f32[2,128,128]{2,1,0:T(8,128)}) async-done(((f32[2,512,128]{2,1,0:T(8,128)}, f32[2,128,128]{2,1,0:T(8,128)}, f32[2,128,128]{2,1,0:T(8,128)}), (f32[2,512,128]{2,1,0:T(8,128)}, f32[2,128,128]{2,1,0:T(8,128)}, f32[2,128,128]{2,1,0:T(8,128)})) %all-reduce.4.cloned.1.call-update) | async-done | bytes 786448 | tf_op jit(solution)/shard_map/psum | solution.py:224
  289.4 1.9 broadcast_multiply_fusion
  291.3 0.7 broadcast_multiply_fusion.2
  291.9 0.3 copy-done.2
  292.2 0.7 broadcast_multiply_fusion.1
  (148 shorter events, 11.7 us)
Async XLA Ops:
  7.2 0.9 copy-start
  8.2 0.7 copy-start.6
  8.9 0.7 copy-start.7
  8.9 0.7 copy-start.8
  9.7 8.3 %copy-start.4 = (bf16[2,512,128]{2,1,0:T(8,128)(2,1)S(1)}, bf16[2,512,128]{2,1,0:T(8,128)(2,1)}, u32[]{:S(2)}) copy-start(bf16[2,512,128]{2,1,0:T(8,128)(2,1)} %param.11) | copy-start | bytes 786436
  11.7 11.9 %all-to-all-start = ((bf16[4,2,1024]{2,1,0:T(2,128)(2,1)}), bf16[4,2,1024]{2,1,0:T(2,128)(2,1)S(1)}, u32[]{:S(2)}, u32[]{:S(2)}) async-start(bf16[4,2,1024]{2,1,0:T(2,128)(2,1)} %reshape.421), calls=%async_computation | async-start | bytes 32768 | tf_op jit(solution)/shard_map/all_to_all | solution.py:70
  23.7 8.8 %all-to-all-start.1 = ((bf16[4,2,1024]{2,1,0:T(2,128)(2,1)}), bf16[4,2,1024]{2,1,0:T(2,128)(2,1)S(1)}, u32[]{:S(2)}, u32[]{:S(2)}) async-start(bf16[4,2,1024]{2,1,0:T(2,128)(2,1)} %reshape.423), calls=%async_computation.1 | async-start | bytes 32768 | tf_op jit(solution)/shard_map/all_to_all | solution.py:72
  33.8 3.4 %copy-start.9 = (f32[2,2,128]{2,1,0:T(2,128)S(1)}, f32[2,2,128]{2,1,0:T(2,128)}, u32[]{:S(2)}) copy-start(f32[2,2,128]{2,1,0:T(2,128)} %param.15) | copy-start | bytes 6148
  33.8 9.0 %all-to-all-start.2 = ((bf16[4,2,1024]{2,1,0:T(2,128)(2,1)}), bf16[4,2,1024]{2,1,0:T(2,128)(2,1)S(1)}, u32[]{:S(2)}, u32[]{:S(2)}) async-start(bf16[4,2,1024]{2,1,0:T(2,128)(2,1)} %reshape.425), calls=%async_computation.2 | async-start | bytes 32768 | tf_op jit(solution)/shard_map/all_to_all | solution.py:81
  43.9 0.8 copy-start.5
  43.9 1.0 copy-start.10
  46.7 8.8 %all-to-all-start.3 = ((bf16[4,2,1024]{2,1,0:T(2,128)(2,1)}), bf16[4,2,1024]{2,1,0:T(2,128)(2,1)S(1)}, u32[]{:S(2)}, u32[]{:S(2)}) async-start(bf16[4,2,1024]{2,1,0:T(2,128)(2,1)} %reshape.429), calls=%async_computation.3 | async-start | bytes 32768 | tf_op jit(solution)/shard_map/all_to_all | solution.py:72
  55.6 8.8 %all-to-all-start.4 = ((bf16[4,2,1024]{2,1,0:T(2,128)(2,1)}), bf16[4,2,1024]{2,1,0:T(2,128)(2,1)S(1)}, u32[]{:S(2)}, u32[]{:S(2)}) async-start(bf16[4,2,1024]{2,1,0:T(2,128)(2,1)} %reshape.427), calls=%async_computation.4 | async-start | bytes 32768 | tf_op jit(solution)/shard_map/all_to_all | solution.py:70
  66.0 3.4 %copy-start.1 = (bf16[1,128,4,16]{1,3,2,0:T(8,128)(2,1)S(1)}, bf16[1,128,4,16]{1,3,2,0:T(8,128)(2,1)}, u32[]{:S(2)}) copy-start(bf16[1,128,4,16]{1,3,2,0:T(8,128)(2,1)} %param.10) | copy-start | bytes 49156
  66.0 9.0 %all-to-all-start.5 = ((bf16[4,2,1024]{2,1,0:T(2,128)(2,1)}), bf16[4,2,1024]{2,1,0:T(2,128)(2,1)S(1)}, u32[]{:S(2)}, u32[]{:S(2)}) async-start(bf16[4,2,1024]{2,1,0:T(2,128)(2,1)} %reshape.431), calls=%async_computation.5 | async-start | bytes 32768 | tf_op jit(solution)/shard_map/all_to_all | solution.py:81
  78.4 8.8 %all-to-all-start.6 = ((bf16[4,2,1024]{2,1,0:T(2,128)(2,1)}), bf16[4,2,1024]{2,1,0:T(2,128)(2,1)S(1)}, u32[]{:S(2)}, u32[]{:S(2)}) async-start(bf16[4,2,1024]{2,1,0:T(2,128)(2,1)} %reshape.433), calls=%async_computation.6 | async-start | bytes 32768 | tf_op jit(solution)/shard_map/all_to_all | solution.py:142
  88.6 8.8 %all-to-all-start.7 = ((bf16[4,2,1024]{2,1,0:T(2,128)(2,1)}), bf16[4,2,1024]{2,1,0:T(2,128)(2,1)S(1)}, u32[]{:S(2)}, u32[]{:S(2)}) async-start(bf16[4,2,1024]{2,1,0:T(2,128)(2,1)} %reshape.437), calls=%async_computation.7 | async-start | bytes 32768 | tf_op jit(solution)/shard_map/all_to_all | solution.py:160
  97.4 8.8 %all-to-all-start.8 = ((bf16[4,2,1024]{2,1,0:T(2,128)(2,1)}), bf16[4,2,1024]{2,1,0:T(2,128)(2,1)S(1)}, u32[]{:S(2)}, u32[]{:S(2)}) async-start(bf16[4,2,1024]{2,1,0:T(2,128)(2,1)} %reshape.435), calls=%async_computation.8 | async-start | bytes 32768 | tf_op jit(solution)/shard_map/all_to_all | solution.py:161
  108.9 8.8 %all-to-all-start.9 = ((bf16[4,2,1024]{2,1,0:T(2,128)(2,1)}), bf16[4,2,1024]{2,1,0:T(2,128)(2,1)S(1)}, u32[]{:S(2)}, u32[]{:S(2)}) async-start(bf16[4,2,1024]{2,1,0:T(2,128)(2,1)} %reshape.439), calls=%async_computation.9 | async-start | bytes 32768 | tf_op jit(solution)/shard_map/all_to_all | solution.py:142
  119.1 8.8 %all-to-all-start.10 = ((bf16[4,2,1024]{2,1,0:T(2,128)(2,1)}), bf16[4,2,1024]{2,1,0:T(2,128)(2,1)S(1)}, u32[]{:S(2)}, u32[]{:S(2)}) async-start(bf16[4,2,1024]{2,1,0:T(2,128)(2,1)} %reshape.443), calls=%async_computation.10 | async-start | bytes 32768 | tf_op jit(solution)/shard_map/all_to_all | solution.py:160
  127.9 8.8 %all-to-all-start.11 = ((bf16[4,2,1024]{2,1,0:T(2,128)(2,1)}), bf16[4,2,1024]{2,1,0:T(2,128)(2,1)S(1)}, u32[]{:S(2)}, u32[]{:S(2)}) async-start(bf16[4,2,1024]{2,1,0:T(2,128)(2,1)} %reshape.441), calls=%async_computation.11 | async-start | bytes 32768 | tf_op jit(solution)/shard_map/all_to_all | solution.py:161
  131.2 158.2 %all-reduce.4.cloned.1.call-start = ((), (), s32[]{:S(2)}) async-start(), calls=%async_computation.12 | async-start | bytes 1572864 | tf_op jit(solution)/shard_map/psum | solution.py:224
  289.4 1.9 copy-start.3
  291.3 1.0 copy-start.2
Sparse Core Ops, SparseCore 0:
  199.6 89.6 all-reduce.3
where the time goes:
time: 301 us; the launch traced here: 300 us
  waiting for transfers between devices  149 us (50%)
  blocking collectives  57.6 us (19%)
  starting transfers between devices  42.4 us (14%)
  local copies, waits for them, and re-layouts  17.4 us (6%)
  between operations  14.8 us (5%)
  other arithmetic  12.5 us (4%)
  matrix products  6.18 us (2%)
    psum x1, waiting for transfers between devices, body(): lax.psum((joined[0], joined[1], joined[2], joined[3], joined[4], joined[5...  89.1 us
    psum x1, blocking collectives, body(): lax.psum((joined[0], joined[1], joined[2], joined[3], joined[4], joined[5...  57.6 us
    unnamed x46, local copies, waits for them, and re-layouts  12.9 us
    all_to_all x2, waiting for transfers between devices, backward_update(): lax.all_to_all(right_term(), 'dap', split_axis=1, concat_axis=0, tiled=True)  10.5 us
    all_to_all x2, waiting for transfers between devices, backward_update(): lax.all_to_all(grad_tri.astype(jnp.bfloat16).reshape(channels, rows, widt...  10.3 us
    all_to_all x2, waiting for transfers between devices, forward_update(): lax.all_to_all(triangle.astype(jnp.bfloat16), 'dap', split_axis=1, concat...  10.3 us
    all_to_all x2, waiting for transfers between devices, forward_update(): lax.all_to_all(right_rows, 'dap', split_axis=0, concat_axis=1, tiled=True)  10 us
    all_to_all x2, starting transfers between devices, forward_update(): lax.all_to_all(left_rows, 'dap', split_axis=0, concat_axis=1, tiled=True)  9.57 us
  transfers between devices with their start and end apart: 13, of which 13 were waited for; matrix products, arithmetic and copies ran while one was open for 3% of the time, Pallas kernels for 0%

commit v1 on v0

--- a/solution.py
+++ b/solution.py
@@ -1,6 +1,10 @@
+import functools
+
 import jax
 import jax.numpy as jnp
 from jax import lax
+from jax.experimental import pallas as pl
+from jax.experimental.pallas import tpu as pltpu
 from jax.sharding import PartitionSpec as P
 
 EPSILON = 1e-05
@@ -192,7 +196,7 @@
     return (upstream + grad_source, grads)
 
 
-def body(
+def large_body(
     pair,
     cotangent,
     proj_weight,
@@ -237,6 +241,426 @@
     )
 
 
+def norm_lanes(values, scale_by, offset):
+    average = jnp.mean(values, axis=1, keepdims=True)
+    centred = values - average
+    variance = jnp.mean(centred * centred, axis=1, keepdims=True)
+    inverse = lax.rsqrt(variance + EPSILON)
+    standard = centred * inverse
+    return (standard * scale_by + offset, standard, inverse)
+
+
+def norm_lanes_back(upstream, scale_by, standard, inverse):
+    scaled = upstream * scale_by
+    adjusted = (
+        scaled
+        - jnp.mean(scaled, axis=1, keepdims=True)
+        - standard * jnp.mean(scaled * standard, axis=1, keepdims=True)
+    )
+    return inverse * adjusted
+
+
+def column_sum(values):
+    return jnp.sum(values, axis=0, keepdims=True)
+
+
+def rounded(values):
+    return values.astype(jnp.bfloat16).astype(jnp.float32)
+
+
+def products(width, a_ref, a_turned, b_ref, b_turned, o_ref):
+    blocks = [
+        b_ref[pl.ds(m, width, stride=width), :] if b_turned else b_ref[pl.ds(m * width, width), :]
+        for m in range(width)
+    ]
+
+    def step(p, carry):
+        total = None
+        for m in range(width):
+            row = a_ref[pl.ds(m * width + p if a_turned else p * width + m, 1), :]
+            term = row * blocks[m]
+            total = term if total is None else total + term
+        o_ref[pl.ds(pl.multiple_of(p * width, width), width), :] = total
+        return carry
+
+    lax.fori_loop(0, width, step, 0)
+
+
+def fused_kernel(
+    peers,
+    width,
+    pair_ref,
+    cot_ref,
+    proj_ref,
+    gate_ref,
+    outw_ref,
+    bias_ref,
+    chan_ref,
+    gain_ref,
+    shift_ref,
+    dpair_ref,
+    big_ref,
+    small_ref,
+    pair_all,
+    cot_all,
+    left_s,
+    right_s,
+    tri_s,
+    grad_s,
+    dleft_s,
+    dright_s,
+    rows_s,
+    send_half,
+    recv_half,
+    send_sum,
+    recv_sum,
+    small_all,
+    gather_send,
+    gather_recv,
+    half_send,
+    half_recv,
+    sum_send,
+    sum_recv,
+    share_send,
+    share_recv,
+    small_send,
+    small_recv,
+):
+    dap, dp = peers
+    mesh_ids = pl.DeviceIdType.MESH
+    channels = pair_ref.shape[1]
+    held = pair_ref.shape[0]
+    me = lax.axis_index("dap")
+    at = lax.axis_index("dp")
+    core = lax.rem(at, 2)
+    core_peer = at + 1 - 2 * core
+    far_peer = lax.rem(at + 2, dp)
+
+    barrier = pltpu.get_barrier_semaphore()
+    for k in range(1, dap):
+        pl.semaphore_signal(
+            barrier, inc=1, device_id={"dap": lax.rem(me + k, dap)}, device_id_type=mesh_ids
+        )
+    for k in range(1, dp):
+        pl.semaphore_signal(
+            barrier, inc=1, device_id={"dp": lax.rem(at + k, dp)}, device_id_type=mesh_ids
+        )
+    pl.semaphore_wait(barrier, dap + dp - 2)
+
+    own = pl.ds(pl.multiple_of(me * held, held), held)
+    gathers = []
+    for slot, (source, whole) in enumerate(((pair_ref, pair_all), (cot_ref, cot_all))):
+        copies = []
+        for k in range(1, dap):
+            copy = pltpu.make_async_remote_copy(
+                src_ref=source,
+                dst_ref=whole.at[own],
+                send_sem=gather_send.at[slot, k - 1],
+                recv_sem=gather_recv.at[slot, k - 1],
+                device_id={"dap": lax.rem(me + k, dap)},
+                device_id_type=mesh_ids,
+            )
+            copy.start()
+            copies.append(copy)
+        gathers.append(copies)
+        whole[own, :] = source[...]
+
+    factor = 1.0 / width
+
+    def forward(source, layer):
+        normed, standard_in, inverse_in = norm_lanes(
+            source, gain_ref[layer, 0:1, :], shift_ref[layer, 0:1, :]
+        )
+        inputs = normed.astype(jnp.bfloat16)
+        pre_act = matmul_rows(inputs, proj_ref[layer]) + bias_ref[layer : layer + 1, :]
+        left_value = pre_act[:, :channels]
+        left_sig = jax.nn.sigmoid(pre_act[:, channels : 2 * channels])
+        right_value = pre_act[:, 2 * channels : 3 * channels]
+        right_sig = jax.nn.sigmoid(pre_act[:, 3 * channels :])
+        left_s[layer] = rounded(left_sig * left_value)
+        right_s[layer] = rounded(right_sig * right_value)
+        gate = jax.nn.sigmoid(matmul_rows(inputs, gate_ref[layer]) + chan_ref[layer, 0:1, :])
+        left, right = left_s.at[layer], right_s.at[layer]
+        if layer == 0:
+            products(width, left, False, right, True, tri_s)
+        else:
+            products(width, left, True, right, False, tri_s)
+        normed_tri, standard_out, inverse_out = norm_lanes(
+            rounded(tri_s[...]), gain_ref[layer, 1:2, :], shift_ref[layer, 1:2, :]
+        )
+        tri_inputs = normed_tri.astype(jnp.bfloat16)
+        linear = matmul_rows(tri_inputs, outw_ref[layer]) + chan_ref[layer, 1:2, :]
+        saved = (
+            inputs,
+            standard_in,
+            inverse_in,
+            left_value,
+            left_sig,
+            right_value,
+            right_sig,
+            gate,
+            linear,
+            tri_inputs,
+            standard_out,
+            inverse_out,
+        )
+        return saved
+
+    def put_small(layer, row, values):
+        rows_s[layer, row : row + 1, :] = values * factor
+
+    def backward_near(upstream, saved, layer):
+        inputs, _, _, _, _, _, _, gate, linear, tri_inputs, standard_out, inverse_out = saved
+        grad_linear = (upstream * gate).astype(jnp.bfloat16)
+        grad_logit = (upstream * linear * gate * (1.0 - gate)).astype(jnp.bfloat16)
+        grad_normed = jnp.dot(grad_linear, outw_ref[layer], preferred_element_type=jnp.float32)
+        grad_s[...] = rounded(
+            norm_lanes_back(grad_normed, gain_ref[layer, 1:2, :], standard_out, inverse_out)
+        )
+        big_ref[layer, 4 * channels : 5 * channels, :] = matmul_cols(grad_logit, inputs) * factor
+        big_ref[layer, 5 * channels :, :] = matmul_cols(grad_linear, tri_inputs) * factor
+        put_small(layer, 4, column_sum(grad_logit.astype(jnp.float32)))
+        put_small(layer, 5, column_sum(grad_linear.astype(jnp.float32)))
+        put_small(layer, 7, column_sum(grad_normed * standard_out))
+        put_small(layer, 9, column_sum(grad_normed))
+        return grad_logit
+
+    def backward_far(upstream, saved, grad_logit, layer):
+        inputs, standard_in, inverse_in, left_value, left_sig, right_value, right_sig = saved[:7]
+        left, right = left_s.at[layer], right_s.at[layer]
+        if layer == 0:
+            products(width, grad_s, False, right, False, dleft_s)
+            products(width, grad_s, True, left, False, dright_s)
+        else:
+            products(width, right, False, grad_s, True, dleft_s)
+            products(width, left, False, grad_s, False, dright_s)
+        left_back = rounded(dleft_s[...])
+        right_back = rounded(dright_s[...])
+        blocks = (
+            left_back * left_sig,
+            left_back * left_value * left_sig * (1.0 - left_sig),
+            right_back * right_sig,
+            right_back * right_value * right_sig * (1.0 - right_sig),
+        )
+        grad_inputs = jnp.dot(grad_logit, gate_ref[layer], preferred_element_type=jnp.float32)
+        for index, block in enumerate(blocks):
+            part = block.astype(jnp.bfloat16)
+            lines = slice(index * channels, (index + 1) * channels)
+            big_ref[layer, lines, :] = matmul_cols(part, inputs) * factor
+            put_small(layer, index, column_sum(part.astype(jnp.float32)))
+            grad_inputs = grad_inputs + jnp.dot(
+                part, proj_ref[layer, lines, :], preferred_element_type=jnp.float32
+            )
+        put_small(layer, 6, column_sum(grad_inputs * standard_in))
+        put_small(layer, 8, column_sum(grad_inputs))
+        return upstream + norm_lanes_back(
+            grad_inputs, gain_ref[layer, 0:1, :], standard_in, inverse_in
+        )
+
+    pieces = (
+        (1, 0, 6 * channels),
+        (0, 4 * channels, 2 * channels),
+        (0, 0, 4 * channels),
+    )
+    flights = {}
+
+    def spans(index):
+        layer, first, count = pieces[index]
+        half = count // 2
+        mine = pl.ds(pl.multiple_of(first + core * half, half), half)
+        other = pl.ds(pl.multiple_of(first + (1 - core) * half, half), half)
+        slot = pl.ds(sum(piece[2] // 2 for piece in pieces[:index]), half)
+        return (big_ref.at[layer], mine, other, slot)
+
+    def exchange_half(index):
+        whole, mine, other, slot = spans(index)
+        send_half[slot, :] = whole[other, :].astype(jnp.bfloat16)
+        copy = pltpu.make_async_remote_copy(
+            src_ref=send_half.at[slot],
+            dst_ref=recv_half.at[slot],
+            send_sem=half_send.at[index],
+            recv_sem=half_recv.at[index],
+            device_id={"dp": core_peer},
+            device_id_type=mesh_ids,
+        )
+        copy.start()
+        flights[index] = [copy]
+
+    def exchange_sum(index):
+        whole, mine, other, slot = spans(index)
+        flights[index][0].wait_recv()
+        added = whole[mine, :] + recv_half[slot, :].astype(jnp.float32)
+        send_sum[slot, :] = added.astype(jnp.bfloat16)
+        copy = pltpu.make_async_remote_copy(
+            src_ref=send_sum.at[slot],
+            dst_ref=recv_sum.at[slot],
+            send_sem=sum_send.at[index],
+            recv_sem=sum_recv.at[index],
+            device_id={"dp": far_peer},
+            device_id_type=mesh_ids,
+        )
+        copy.start()
+        flights[index].append(copy)
+
+    def share(index):
+        whole, mine, other, slot = spans(index)
+        flights[index][1].wait_recv()
+        whole[mine, :] = send_sum[slot, :].astype(jnp.float32) + recv_sum[slot, :].astype(
+            jnp.float32
+        )
+        copy = pltpu.make_async_remote_copy(
+            src_ref=whole.at[mine],
+            dst_ref=whole.at[mine],
+            send_sem=share_send.at[index],
+            recv_sem=share_recv.at[index],
+            device_id={"dp": core_peer},
+            device_id_type=mesh_ids,
+        )
+        copy.start()
+        flights[index].append(copy)
+
+    for copy in gathers[0]:
+        copy.wait_recv()
+    start_pair = pair_all[...].astype(jnp.float32)
+    saved_first = forward(start_pair, 0)
+    middle = rounded(start_pair + saved_first[7] * saved_first[8])
+    saved_second = forward(middle, 1)
+    for copy in gathers[1]:
+        copy.wait_recv()
+    upstream = cot_all[...].astype(jnp.float32)
+    grad_logit = backward_near(upstream, saved_second, 1)
+    grad_middle = backward_far(upstream, saved_second, grad_logit, 1)
+    exchange_half(0)
+    grad_logit = backward_near(grad_middle, saved_first, 0)
+    exchange_half(1)
+    exchange_sum(0)
+    grad_start = backward_far(grad_middle, saved_first, grad_logit, 0)
+    exchange_half(2)
+    small_all[at] = rows_s[...]
+    small_copies = []
+    for k in range(1, dp):
+        copy = pltpu.make_async_remote_copy(
+            src_ref=rows_s,
+            dst_ref=small_all.at[at],
+            send_sem=small_send.at[k - 1],
+            recv_sem=small_recv.at[k - 1],
+            device_id={"dp": lax.rem(at + k, dp)},
+            device_id_type=mesh_ids,
+        )
+        copy.start()
+        small_copies.append(copy)
+    exchange_sum(1)
+    exchange_sum(2)
+    dleft_s[...] = grad_start
+    dpair_ref[...] = dleft_s[own, :].astype(jnp.bfloat16)
+    share(0)
+    share(1)
+    for copy in small_copies:
+        copy.wait_recv()
+    total = small_all[0]
+    for index in range(1, dp):
+        total = total + small_all[index]
+    small_ref[...] = total
+    share(2)
+    for index in range(3):
+        flights[index][2].wait_recv()
+    for index in range(3):
+        for copy in flights[index]:
+            copy.wait_send()
+    for copy in gathers[0] + gathers[1] + small_copies:
+        copy.wait_send()
+
+
+def fused_body(
+    peers,
+    pair,
+    cotangent,
+    proj_weight,
+    proj_bias,
+    gate_weight,
+    out_weight,
+    chan_bias,
+    norm_gain,
+    norm_shift,
+):
+    dap, dp = peers
+    _, channels, rows, width = pair.shape
+    held = rows * width
+    entries = width * width
+    float_rows = pltpu.VMEM((entries, channels), jnp.float32)
+    layer_rows = pltpu.VMEM((2, entries, channels), jnp.float32)
+    half_rows = pltpu.VMEM((6 * channels, channels), jnp.bfloat16)
+    vmem = pl.BlockSpec(memory_space=pltpu.VMEM)
+    grad_rows, big, small = pl.pallas_call(
+        functools.partial(fused_kernel, peers, width),
+        out_shape=(
+            jax.ShapeDtypeStruct((held, channels), jnp.bfloat16),
+            jax.ShapeDtypeStruct((2, 6 * channels, channels), jnp.float32),
+            jax.ShapeDtypeStruct((2, 10, channels), jnp.float32),
+        ),
+        in_specs=[vmem] * 9,
+        out_specs=(vmem, vmem, vmem),
+        scratch_shapes=[
+            pltpu.VMEM((entries, channels), jnp.bfloat16),
+            pltpu.VMEM((entries, channels), jnp.bfloat16),
+            layer_rows,
+            layer_rows,
+            float_rows,
+            float_rows,
+            float_rows,
+            float_rows,
+            pltpu.VMEM((2, 10, channels), jnp.float32),
+            half_rows,
+            half_rows,
+            half_rows,
+            half_rows,
+            pltpu.VMEM((dp, 2, 10, channels), jnp.float32),
+            pltpu.SemaphoreType.DMA((2, dap - 1)),
+            pltpu.SemaphoreType.DMA((2, dap - 1)),
+            pltpu.SemaphoreType.DMA((3,)),
+            pltpu.SemaphoreType.DMA((3,)),
+            pltpu.SemaphoreType.DMA((3,)),
+            pltpu.SemaphoreType.DMA((3,)),
+            pltpu.SemaphoreType.DMA((3,)),
+            pltpu.SemaphoreType.DMA((3,)),
+            pltpu.SemaphoreType.DMA((dp - 1,)),
+            pltpu.SemaphoreType.DMA((dp - 1,)),
+        ],
+        compiler_params=pltpu.CompilerParams(
+            collective_id=0, has_side_effects=True, vmem_limit_bytes=40 * 1024 * 1024
+        ),
+        name="triangle_updates",
+    )(
+        pair[0].reshape(channels, held).T,
+        cotangent[0].reshape(channels, held).T,
+        proj_weight,
+        gate_weight,
+        out_weight,
+        proj_bias,
+        chan_bias,
+        norm_gain,
+        norm_shift,
+    )
+    return (
+        grad_rows.T.reshape(1, channels, rows, width),
+        big[:, : 4 * channels],
+        small[:, :4].reshape(2, 4 * channels),
+        big[:, 4 * channels : 5 * channels],
+        big[:, 5 * channels :],
+        small[:, 4:6],
+        small[:, 6:8],
+        small[:, 8:10],
+    )
+
+
+def any_body(peers, pair, *others):
+    _, channels, rows, width = pair.shape
+    small = channels == 128 and width == 16 and rows % 4 == 0
+    if small and peers[1] == 4 and peers[0] > 1:
+        return fused_body(peers, pair, *others)
+    return large_body(pair, *others)
+
+
 def solution(mesh):
     in_specs = (
         P(("groups", "dp"), None, "dap", None),
@@ -259,4 +683,6 @@
         P("groups", None, None),
         P("groups", None, None),
     )
+    peers = (mesh.shape["dap"], mesh.shape["dp"])
+    body = functools.partial(any_body, peers)
     return jax.shard_map(body, mesh=mesh, in_specs=in_specs, out_specs=out_specs, check_vma=False)

time: 301 us -> 31.8 us (0.11)
  waiting for transfers between devices: 149 us -> 0 us
  blocking collectives: 57.6 us -> 0 us
  starting transfers between devices: 42.4 us -> 0 us
  Pallas kernels: 0 us -> 20.6 us
  between operations: 14.8 us -> 0.67 us
  other arithmetic: 12.5 us -> 0 us
  local copies, waits for them, and re-layouts: 17.4 us -> 10.1 us
  matrix products: 6.18 us -> 0 us
    psum x1 -> x0, waiting for transfers between devices: 89.1 us -> none  [body(): lax.psum((joined[0], joined[1], joined[2], joined[3], joined[4], joined[5...]
    all_to_all x12 -> x0, waiting for transfers between devices: 59.6 us -> none  [the longest x2 10.5 us: backward_update(): lax.all_to_all(right_term(), 'dap', split_axis=1, concat_axis=0, tiled=True)]
    psum x1 -> x0, blocking collectives: 57.6 us -> none  [body(): lax.psum((joined[0], joined[1], joined[2], joined[3], joined[4], joined[5...]
    all_to_all x12 -> x0, starting transfers between devices: 42.4 us -> none  [the longest x2 9.57 us: forward_update(): lax.all_to_all(left_rows, 'dap', split_axis=0, concat_axis=1, tiled=True)]
    pallas_call x0 -> x1, Pallas kernels: none -> 20.6 us  [fused_body(): pl.pallas_call(functools.partial(fused_kernel, peers, width), out_shape=(...]
    dot_general x26 -> x0, matrix products: 6.18 us -> none  [the longest x4 1.57 us: gated(): jnp.dot(weight_now[first_row:first_row + 2 * channels], inputs, preferred...]
    mul x7 -> x0, other arithmetic: 5.57 us -> none  [the longest x1 1.9 us: body(): stacked[0] * factor]
    unnamed x46 -> x21, local copies, waits for them, and re-layouts: 12.9 us -> 7.99 us
  transfers between devices with their start and end apart: 13 -> 0, of which waited for: 13 -> 0; matrix products, arithmetic and copies ran while one was open for 3% -> 0% of each run, Pallas kernels for 0% -> 0%
where the time goes in v1:
time: 31.8 us; the launch traced here: 31.4 us
  Pallas kernels  20.6 us (65%)
  local copies, waits for them, and re-layouts  10.1 us (32%)
  between operations  0.67 us (2%)
    pallas_call x1, Pallas kernels, fused_body(): pl.pallas_call(functools.partial(fused_kernel, peers, width), out_shape=(...  20.6 us
    unnamed x21, local copies, waits for them, and re-layouts  7.99 us
    slice x1, local copies, waits for them, and re-layouts, fused_body(): big[:, :4 * channels]  0.83 us
    slice x1, local copies, waits for them, and re-layouts, fused_body(): big[:, 5 * channels:]  0.72 us

profile of v1, /device:TPU:0, one launch (start us, length us, event | category | flops | bytes accessed | tf_op | source)
XLA Modules:
  0.0 31.4 jit_solution(11439883424368021755)
XLA Ops:
  0.6 0.0 copy-start.6
  0.6 0.7 %copy-done.6 = f32[2,2,128]{2,1,0:T(2,128)S(1)} copy-done((f32[2,2,128]{2,1,0:T(2,128)S(1)}, f32[2,2,128]{2,1,0:T(2,128)}, u32[]{:S(2)}) %copy-start.6) | copy-done | bytes 2072
  1.3 0.0 copy-start
  1.3 0.9 %copy-done = bf16[2,512,128]{2,1,0:T(8,128)(2,1)S(1)} copy-done((bf16[2,512,128]{2,1,0:T(8,128)(2,1)S(1)}, bf16[2,512,128]{2,1,0:T(8,128)(2,1)}, u32[]{:S(2)}) %copy-start) | copy-done | bytes 262168
  2.3 0.0 copy-start.1
  2.3 0.8 %copy-done.1 = bf16[2,128,128]{2,1,0:T(8,128)(2,1)S(1)} copy-done((bf16[2,128,128]{2,1,0:T(8,128)(2,1)S(1)}, bf16[2,128,128]{2,1,0:T(8,128)(2,1)}, u32[]{:S(2)}) %copy-start.1) | copy-done | bytes 65560
  3.1 0.0 copy-start.2
  3.1 0.8 %copy-done.2 = bf16[2,128,128]{2,1,0:T(8,128)(2,1)S(1)} copy-done((bf16[2,128,128]{2,1,0:T(8,128)(2,1)S(1)}, bf16[2,128,128]{2,1,0:T(8,128)(2,1)}, u32[]{:S(2)}) %copy-start.2) | copy-done | bytes 65560
  3.9 0.0 copy-start.3
  4.0 0.7 %copy-done.3 = bf16[1,128,4,16]{1,3,2,0:T(8,128)(2,1)S(1)} copy-done((bf16[1,128,4,16]{1,3,2,0:T(8,128)(2,1)S(1)}, bf16[1,128,4,16]{1,3,2,0:T(8,128)(2,1)}, u32[]{:S(2)}) %copy-start.3) | copy-done | bytes 16408
  4.7 0.0 copy-start.4
  4.7 0.7 %copy-done.4 = bf16[1,128,4,16]{1,3,2,0:T(8,128)(2,1)S(1)} copy-done((bf16[1,128,4,16]{1,3,2,0:T(8,128)(2,1)S(1)}, bf16[1,128,4,16]{1,3,2,0:T(8,128)(2,1)}, u32[]{:S(2)}) %copy-start.4) | copy-done | bytes 16408
  5.4 0.0 copy-start.5
  5.4 0.7 %copy-done.5 = f32[2,512]{1,0:T(2,128)S(1)} copy-done((f32[2,512]{1,0:T(2,128)S(1)}, f32[2,512]{1,0:T(2,128)}, u32[]{:S(2)}) %copy-start.5) | copy-done | bytes 4120
  6.1 0.0 copy-start.7
  6.1 0.7 %copy-done.7 = f32[2,2,128]{2,1,0:T(2,128)S(1)} copy-done((f32[2,2,128]{2,1,0:T(2,128)S(1)}, f32[2,2,128]{2,1,0:T(2,128)}, u32[]{:S(2)}) %copy-start.7) | copy-done | bytes 2072
  6.8 0.0 copy-start.8
  6.8 0.7 %copy-done.8 = f32[2,2,128]{2,1,0:T(2,128)S(1)} copy-done((f32[2,2,128]{2,1,0:T(2,128)S(1)}, f32[2,2,128]{2,1,0:T(2,128)}, u32[]{:S(2)}) %copy-start.8) | copy-done | bytes 2072
  7.4 20.6 %triangle_updates.1 = (bf16[64,128]{1,0:T(8,128)(2,1)S(1)}, f32[2,768,128]{2,1,0:T(8,128)S(1)}, f32[2,10,128]{2,1,0:T(8,128)S(1)}) custom-call(bf16[64,128]{1,0:T(8,128)(2,1)S(1)} %bitcast.15, bf16[64,128]{1,0:T(8,128)(2,1)S(1)} %bitcast.16, bf16[2,512,128]{2,1,0:T(8,128)(2,1)S(1)} %copy-done, bf16[2,128,128]{2,1,0:T(8,128)(2,1)S(1)} %copy-done.1, ...), custom_call_target="tpu_custom_call" | custom-call | tf_op jit(solution)/shard_map/triangle_updates/pallas_call | solution.py:594
  28.1 0.6 %fusion.1 = (f32[2,2,128]{2,1,0:T(2,128)}, f32[2,2,128]{2,1,0:T(2,128)}, f32[2,2,128]{2,1,0:T(2,128)}) fusion(f32[2,10,128]{2,1,0:T(8,128)S(1)} %get-tuple-element.13), kind=kLoop, calls=%fused_computation.3 | loop fusion | bytes 12288 | tf_op jit(solution)/shard_map/slice | solution.py:652
  28.7 0.6 %copy.19 = f32[1,2,4,128]{3,1,2,0:T(2,128)} copy(f32[1,2,4,128]{3,2,1,0:T(4,128)S(1)} %slice_bitcast_fusion) | data formatting | bytes 8192
  29.3 0.7 %fusion = (f32[2,128,128]{2,1,0:T(8,128)}, f32[2,128,128]{2,1,0:T(8,128)}) fusion(f32[2,768,128]{2,1,0:T(8,128)S(1)} %get-tuple-element.12), kind=kLoop, calls=%fused_computation.2 | loop fusion | bytes 524288 | tf_op jit(solution)/shard_map/slice | solution.py:649
  30.0 0.8 %slice.21 = f32[2,512,128]{2,1,0:T(8,128)} slice(f32[2,768,128]{2,1,0:T(8,128)S(1)} %get-tuple-element.12), slice={[0:2], [0:512], [0:128]} | slice | bytes 1048576 | tf_op jit(solution)/shard_map/slice | solution.py:646
  30.8 0.6 %copy.21 = bf16[1,128,4,16]{1,3,2,0:T(8,128)(2,1)} copy(bf16[1,128,4,16]{1,3,2,0:T(8,128)(2,1)S(1)} %bitcast.14) | data formatting | bytes 32768
  (1 shorter events, 0.0 us)
Async XLA Ops:
  0.6 0.7 %copy-start.6 = (f32[2,2,128]{2,1,0:T(2,128)S(1)}, f32[2,2,128]{2,1,0:T(2,128)}, u32[]{:S(2)}) copy-start(f32[2,2,128]{2,1,0:T(2,128)} %chan_ref.1) | copy-start | bytes 6148
  1.3 0.9 %copy-start = (bf16[2,512,128]{2,1,0:T(8,128)(2,1)S(1)}, bf16[2,512,128]{2,1,0:T(8,128)(2,1)}, u32[]{:S(2)}) copy-start(bf16[2,512,128]{2,1,0:T(8,128)(2,1)} %proj_ref.1) | copy-start | bytes 786436
  2.3 0.8 %copy-start.1 = (bf16[2,128,128]{2,1,0:T(8,128)(2,1)S(1)}, bf16[2,128,128]{2,1,0:T(8,128)(2,1)}, u32[]{:S(2)}) copy-start(bf16[2,128,128]{2,1,0:T(8,128)(2,1)} %gate_ref.1) | copy-start | bytes 196612
  3.1 0.8 %copy-start.2 = (bf16[2,128,128]{2,1,0:T(8,128)(2,1)S(1)}, bf16[2,128,128]{2,1,0:T(8,128)(2,1)}, u32[]{:S(2)}) copy-start(bf16[2,128,128]{2,1,0:T(8,128)(2,1)} %outw_ref.1) | copy-start | bytes 196612
  3.9 0.7 %copy-start.3 = (bf16[1,128,4,16]{1,3,2,0:T(8,128)(2,1)S(1)}, bf16[1,128,4,16]{1,3,2,0:T(8,128)(2,1)}, u32[]{:S(2)}) copy-start(bf16[1,128,4,16]{1,3,2,0:T(8,128)(2,1)} %param.9) | copy-start | bytes 49156
  4.7 0.7 %copy-start.4 = (bf16[1,128,4,16]{1,3,2,0:T(8,128)(2,1)S(1)}, bf16[1,128,4,16]{1,3,2,0:T(8,128)(2,1)}, u32[]{:S(2)}) copy-start(bf16[1,128,4,16]{1,3,2,0:T(8,128)(2,1)} %param.10) | copy-start | bytes 49156
  5.4 0.7 %copy-start.5 = (f32[2,512]{1,0:T(2,128)S(1)}, f32[2,512]{1,0:T(2,128)}, u32[]{:S(2)}) copy-start(f32[2,512]{1,0:T(2,128)} %bias_ref.1) | copy-start | bytes 12292
  6.1 0.7 %copy-start.7 = (f32[2,2,128]{2,1,0:T(2,128)S(1)}, f32[2,2,128]{2,1,0:T(2,128)}, u32[]{:S(2)}) copy-start(f32[2,2,128]{2,1,0:T(2,128)} %gain_ref.1) | copy-start | bytes 6148
  6.8 0.7 %copy-start.8 = (f32[2,2,128]{2,1,0:T(2,128)S(1)}, f32[2,2,128]{2,1,0:T(2,128)}, u32[]{:S(2)}) copy-start(f32[2,2,128]{2,1,0:T(2,128)} %shift_ref.1) | copy-start | bytes 6148

commit v2 on v1

--- a/solution.py
+++ b/solution.py
@@ -289,8 +289,27 @@
 def fused_kernel(
     peers,
     width,
-    pair_ref,
-    cot_ref,
+    pair_hbm,
+    cot_hbm,
+    proj_hbm,
+    gate_hbm,
+    outw_hbm,
+    bias_hbm,
+    chan_hbm,
+    gain_hbm,
+    shift_hbm,
+    dpair_out,
+    big_out,
+    dbias_out,
+    dchan_out,
+    dgain_out,
+    dshift_out,
+    dpair_ref,
+    big_ref,
+    dbias_ref,
+    dchan_ref,
+    dgain_ref,
+    dshift_ref,
     proj_ref,
     gate_ref,
     outw_ref,
@@ -298,9 +317,6 @@
     chan_ref,
     gain_ref,
     shift_ref,
-    dpair_ref,
-    big_ref,
-    small_ref,
     pair_all,
     cot_all,
     left_s,
@@ -315,6 +331,8 @@
     send_sum,
     recv_sum,
     small_all,
+    fetch_done,
+    store_done,
     gather_send,
     gather_recv,
     half_send,
@@ -328,14 +346,30 @@
 ):
     dap, dp = peers
     mesh_ids = pl.DeviceIdType.MESH
-    channels = pair_ref.shape[1]
-    held = pair_ref.shape[0]
+    held, channels = pair_hbm.shape
     me = lax.axis_index("dap")
     at = lax.axis_index("dp")
     core = lax.rem(at, 2)
     core_peer = at + 1 - 2 * core
     far_peer = lax.rem(at + 2, dp)
 
+    own = pl.ds(pl.multiple_of(me * held, held), held)
+    fetches = []
+    for source, target in (
+        (pair_hbm, pair_all.at[own]),
+        (cot_hbm, cot_all.at[own]),
+        (gain_hbm, gain_ref),
+        (shift_hbm, shift_ref),
+        (proj_hbm, proj_ref),
+        (bias_hbm, bias_ref),
+        (gate_hbm, gate_ref),
+        (chan_hbm, chan_ref),
+        (outw_hbm, outw_ref),
+    ):
+        copy = pltpu.make_async_copy(source, target, fetch_done.at[len(fetches)])
+        copy.start()
+        fetches.append(copy)
+
     barrier = pltpu.get_barrier_semaphore()
     for k in range(1, dap):
         pl.semaphore_signal(
@@ -347,13 +381,13 @@
         )
     pl.semaphore_wait(barrier, dap + dp - 2)
 
-    own = pl.ds(pl.multiple_of(me * held, held), held)
     gathers = []
-    for slot, (source, whole) in enumerate(((pair_ref, pair_all), (cot_ref, cot_all))):
+    for slot, whole in enumerate((pair_all, cot_all)):
+        fetches[slot].wait()
         copies = []
         for k in range(1, dap):
             copy = pltpu.make_async_remote_copy(
-                src_ref=source,
+                src_ref=whole.at[own],
                 dst_ref=whole.at[own],
                 send_sem=gather_send.at[slot, k - 1],
                 recv_sem=gather_recv.at[slot, k - 1],
@@ -363,7 +397,6 @@
             copy.start()
             copies.append(copy)
         gathers.append(copies)
-        whole[own, :] = source[...]
 
     factor = 1.0 / width
 
@@ -463,6 +496,12 @@
         (0, 0, 4 * channels),
     )
     flights = {}
+    stores = []
+
+    def store(source, target):
+        copy = pltpu.make_async_copy(source, target, store_done.at[len(stores)])
+        copy.start()
+        stores.append(copy)
 
     def spans(index):
         layer, first, count = pieces[index]
@@ -510,7 +549,7 @@
         )
         copy = pltpu.make_async_remote_copy(
             src_ref=whole.at[mine],
-            dst_ref=whole.at[mine],
+            dst_ref=big_out.at[pieces[index][0], mine],
             send_sem=share_send.at[index],
             recv_sem=share_recv.at[index],
             device_id={"dp": core_peer},
@@ -518,7 +557,10 @@
         )
         copy.start()
         flights[index].append(copy)
-
+        store(whole.at[mine], big_out.at[pieces[index][0], mine])
+
+    for copy in fetches[2:]:
+        copy.wait()
     for copy in gathers[0]:
         copy.wait_recv()
     start_pair = pair_all[...].astype(jnp.float32)
@@ -553,6 +595,7 @@
     exchange_sum(2)
     dleft_s[...] = grad_start
     dpair_ref[...] = dleft_s[own, :].astype(jnp.bfloat16)
+    store(dpair_ref, dpair_out)
     share(0)
     share(1)
     for copy in small_copies:
@@ -560,7 +603,15 @@
     total = small_all[0]
     for index in range(1, dp):
         total = total + small_all[index]
-    small_ref[...] = total
+    for index in range(4):
+        dbias_ref[:, index * channels : (index + 1) * channels] = total[:, index]
+    dchan_ref[...] = total[:, 4:6]
+    dgain_ref[...] = total[:, 6:8]
+    dshift_ref[...] = total[:, 8:10]
+    store(dbias_ref, dbias_out)
+    store(dchan_ref, dchan_out)
+    store(dgain_ref, dgain_out)
+    store(dshift_ref, dshift_out)
     share(2)
     for index in range(3):
         flights[index][2].wait_recv()
@@ -569,6 +620,44 @@
             copy.wait_send()
     for copy in gathers[0] + gathers[1] + small_copies:
         copy.wait_send()
+    for copy in stores:
+        copy.wait()
+
+
+def deliver_kernel(
+    dpair_ref,
+    big_ref,
+    dbias_ref,
+    dchan_ref,
+    dgain_ref,
+    dshift_ref,
+    dpair_out,
+    proj_out,
+    bias_out,
+    gate_out,
+    outw_out,
+    chan_out,
+    gain_out,
+    shift_out,
+    done,
+):
+    channels = big_ref.shape[2]
+    copies = []
+    for source, target in (
+        (big_ref.at[:, : 4 * channels], proj_out),
+        (big_ref.at[:, 4 * channels : 5 * channels], gate_out),
+        (big_ref.at[:, 5 * channels :], outw_out),
+        (dpair_ref, dpair_out),
+        (dbias_ref, bias_out),
+        (dchan_ref, chan_out),
+        (dgain_ref, gain_out),
+        (dshift_ref, shift_out),
+    ):
+        copy = pltpu.make_async_copy(source, target, done.at[len(copies)])
+        copy.start()
+        copies.append(copy)
+    for copy in copies:
+        copy.wait()
 
 
 def fused_body(
@@ -590,17 +679,33 @@
     float_rows = pltpu.VMEM((entries, channels), jnp.float32)
     layer_rows = pltpu.VMEM((2, entries, channels), jnp.float32)
     half_rows = pltpu.VMEM((6 * channels, channels), jnp.bfloat16)
-    vmem = pl.BlockSpec(memory_space=pltpu.VMEM)
-    grad_rows, big, small = pl.pallas_call(
+    hbm = pl.BlockSpec(memory_space=pltpu.HBM)
+    summed = pl.pallas_call(
         functools.partial(fused_kernel, peers, width),
         out_shape=(
             jax.ShapeDtypeStruct((held, channels), jnp.bfloat16),
             jax.ShapeDtypeStruct((2, 6 * channels, channels), jnp.float32),
-            jax.ShapeDtypeStruct((2, 10, channels), jnp.float32),
+            jax.ShapeDtypeStruct((2, 4 * channels), jnp.float32),
+            jax.ShapeDtypeStruct((2, 2, channels), jnp.float32),
+            jax.ShapeDtypeStruct((2, 2, channels), jnp.float32),
+            jax.ShapeDtypeStruct((2, 2, channels), jnp.float32),
         ),
-        in_specs=[vmem] * 9,
-        out_specs=(vmem, vmem, vmem),
+        in_specs=[hbm] * 9,
+        out_specs=(hbm,) * 6,
         scratch_shapes=[
+            pltpu.VMEM((held, channels), jnp.bfloat16),
+            pltpu.VMEM((2, 6 * channels, channels), jnp.float32),
+            pltpu.VMEM((2, 4 * channels), jnp.float32),
+            pltpu.VMEM((2, 2, channels), jnp.float32),
+            pltpu.VMEM((2, 2, channels), jnp.float32),
+            pltpu.VMEM((2, 2, channels), jnp.float32),
+            pltpu.VMEM(proj_weight.shape, jnp.bfloat16),
+            pltpu.VMEM(gate_weight.shape, jnp.bfloat16),
+            pltpu.VMEM(out_weight.shape, jnp.bfloat16),
+            pltpu.VMEM(proj_bias.shape, jnp.float32),
+            pltpu.VMEM(chan_bias.shape, jnp.float32),
+            pltpu.VMEM(norm_gain.shape, jnp.float32),
+            pltpu.VMEM(norm_shift.shape, jnp.float32),
             pltpu.VMEM((entries, channels), jnp.bfloat16),
             pltpu.VMEM((entries, channels), jnp.bfloat16),
             layer_rows,
@@ -615,6 +720,8 @@
             half_rows,
             half_rows,
             pltpu.VMEM((dp, 2, 10, channels), jnp.float32),
+            pltpu.SemaphoreType.DMA((9,)),
+            pltpu.SemaphoreType.DMA((8,)),
             pltpu.SemaphoreType.DMA((2, dap - 1)),
             pltpu.SemaphoreType.DMA((2, dap - 1)),
             pltpu.SemaphoreType.DMA((3,)),
@@ -627,7 +734,7 @@
             pltpu.SemaphoreType.DMA((dp - 1,)),
         ],
         compiler_params=pltpu.CompilerParams(
-            collective_id=0, has_side_effects=True, vmem_limit_bytes=40 * 1024 * 1024
+            collective_id=0, has_side_effects=True, vmem_limit_bytes=62 * 1024 * 1024
         ),
         name="triangle_updates",
     )(
@@ -641,16 +748,25 @@
         norm_gain,
         norm_shift,
     )
-    return (
-        grad_rows.T.reshape(1, channels, rows, width),
-        big[:, : 4 * channels],
-        small[:, :4].reshape(2, 4 * channels),
-        big[:, 4 * channels : 5 * channels],
-        big[:, 5 * channels :],
-        small[:, 4:6],
-        small[:, 6:8],
-        small[:, 8:10],
-    )
+    outputs = pl.pallas_call(
+        deliver_kernel,
+        out_shape=(
+            jax.ShapeDtypeStruct((held, channels), jnp.bfloat16),
+            jax.ShapeDtypeStruct((2, 4 * channels, channels), jnp.float32),
+            jax.ShapeDtypeStruct((2, 4 * channels), jnp.float32),
+            jax.ShapeDtypeStruct((2, channels, channels), jnp.float32),
+            jax.ShapeDtypeStruct((2, channels, channels), jnp.float32),
+            jax.ShapeDtypeStruct((2, 2, channels), jnp.float32),
+            jax.ShapeDtypeStruct((2, 2, channels), jnp.float32),
+            jax.ShapeDtypeStruct((2, 2, channels), jnp.float32),
+        ),
+        in_specs=[hbm] * 6,
+        out_specs=(hbm,) * 8,
+        scratch_shapes=[pltpu.SemaphoreType.DMA((8,))],
+        compiler_params=pltpu.CompilerParams(vmem_limit_bytes=62 * 1024 * 1024),
+        name="deliver",
+    )(*summed)
+    return (outputs[0].T.reshape(1, channels, rows, width),) + tuple(outputs[1:])
 
 
 def any_body(peers, pair, *others):

time: 31.8 us -> 47.6 us (1.50)
  Pallas kernels: 20.6 us -> 46.8 us
  local copies, waits for them, and re-layouts: 10.1 us -> 0 us
    pallas_call x0 -> x1, Pallas kernels: none -> 25.8 us  [fused_body(): pl.pallas_call(deliver_kernel, out_shape=(jax.ShapeDtypeStruct((held, cha...]
    unnamed x21 -> x0, local copies, waits for them, and re-layouts: 7.99 us -> none
    slice x3 -> x0, local copies, waits for them, and re-layouts: 2.13 us -> none  [the longest x1 0.83 us: fused_body(): big[:, :4 * channels]]
where the time goes in v2:
time: 47.6 us; the launch traced here: 47.5 us
  Pallas kernels  46.8 us (98%)
  between operations  0.64 us (1%)
    pallas_call x1, Pallas kernels, fused_body(): pl.pallas_call(deliver_kernel, out_shape=(jax.ShapeDtypeStruct((held, cha...  25.8 us
    pallas_call x1, Pallas kernels, fused_body(): pl.pallas_call(functools.partial(fused_kernel, peers, width), out_shape=(...  21 us

profile of v2, /device:TPU:0, one launch (start us, length us, event | category | flops | bytes accessed | tf_op | source)
XLA Modules:
  0.0 47.5 jit_solution(9082383605655592673)
XLA Ops:
  0.6 21.0 %triangle_updates.1 = (bf16[64,128]{1,0:T(8,128)(2,1)}, f32[2,768,128]{2,1,0:T(8,128)}, f32[2,512]{1,0:T(2,128)}, f32[2,2,128]{2,1,0:T(2,128)}, f32[2,2,128]{2,1,0:T(2,128)}, /*index=5*/f32[2,2,128]{2,1,0:T(2,128)}) custom-call(bf16[64,128]{1,0:T(8,128)(2,1)} %bitcast.9, bf16[64,128]{1,0:T(8,128)(2,1)} %bitcast.10, bf16[2,512,128]{2,1,0:T(8,128)(2,1)} %proj_hbm.1, ...), custom_call_target="tpu_custom_call" | custom-call | tf_op jit(solution)/shard_map/triangle_updates/pallas_call | solution.py:683
  21.7 25.8 %deliver.1 = (bf16[64,128]{1,0:T(8,128)(2,1)}, f32[2,512,128]{2,1,0:T(8,128)}, f32[2,512]{1,0:T(2,128)}, f32[2,128,128]{2,1,0:T(8,128)}, f32[2,128,128]{2,1,0:T(...) custom-call(bf16[64,128]{1,0:T(8,128)(2,1)} %get-tuple-element.22.dpair_ref, ...), custom_call_target="tpu_custom_call" | custom-call | tf_op jit(solution)/shard_map/deliver/pallas_call | solution.py:751

commit v3 on v2

--- a/solution.py
+++ b/solution.py
@@ -298,12 +298,6 @@
     chan_hbm,
     gain_hbm,
     shift_hbm,
-    dpair_out,
-    big_out,
-    dbias_out,
-    dchan_out,
-    dgain_out,
-    dshift_out,
     dpair_ref,
     big_ref,
     dbias_ref,
@@ -332,7 +326,6 @@
     recv_sum,
     small_all,
     fetch_done,
-    store_done,
     gather_send,
     gather_recv,
     half_send,
@@ -496,12 +489,6 @@
         (0, 0, 4 * channels),
     )
     flights = {}
-    stores = []
-
-    def store(source, target):
-        copy = pltpu.make_async_copy(source, target, store_done.at[len(stores)])
-        copy.start()
-        stores.append(copy)
 
     def spans(index):
         layer, first, count = pieces[index]
@@ -549,7 +536,7 @@
         )
         copy = pltpu.make_async_remote_copy(
             src_ref=whole.at[mine],
-            dst_ref=big_out.at[pieces[index][0], mine],
+            dst_ref=whole.at[mine],
             send_sem=share_send.at[index],
             recv_sem=share_recv.at[index],
             device_id={"dp": core_peer},
@@ -557,7 +544,6 @@
         )
         copy.start()
         flights[index].append(copy)
-        store(whole.at[mine], big_out.at[pieces[index][0], mine])
 
     for copy in fetches[2:]:
         copy.wait()
@@ -595,7 +581,6 @@
     exchange_sum(2)
     dleft_s[...] = grad_start
     dpair_ref[...] = dleft_s[own, :].astype(jnp.bfloat16)
-    store(dpair_ref, dpair_out)
     share(0)
     share(1)
     for copy in small_copies:
@@ -608,10 +593,6 @@
     dchan_ref[...] = total[:, 4:6]
     dgain_ref[...] = total[:, 6:8]
     dshift_ref[...] = total[:, 8:10]
-    store(dbias_ref, dbias_out)
-    store(dchan_ref, dchan_out)
-    store(dgain_ref, dgain_out)
-    store(dshift_ref, dshift_out)
     share(2)
     for index in range(3):
         flights[index][2].wait_recv()
@@ -620,8 +601,6 @@
             copy.wait_send()
     for copy in gathers[0] + gathers[1] + small_copies:
         copy.wait_send()
-    for copy in stores:
-        copy.wait()
 
 
 def deliver_kernel(
@@ -679,26 +658,21 @@
     float_rows = pltpu.VMEM((entries, channels), jnp.float32)
     layer_rows = pltpu.VMEM((2, entries, channels), jnp.float32)
     half_rows = pltpu.VMEM((6 * channels, channels), jnp.bfloat16)
+    vmem = pl.BlockSpec(memory_space=pltpu.VMEM)
     hbm = pl.BlockSpec(memory_space=pltpu.HBM)
     summed = pl.pallas_call(
         functools.partial(fused_kernel, peers, width),
         out_shape=(
-            jax.ShapeDtypeStruct((held, channels), jnp.bfloat16),
-            jax.ShapeDtypeStruct((2, 6 * channels, channels), jnp.float32),
-            jax.ShapeDtypeStruct((2, 4 * channels), jnp.float32),
-            jax.ShapeDtypeStruct((2, 2, channels), jnp.float32),
-            jax.ShapeDtypeStruct((2, 2, channels), jnp.float32),
-            jax.ShapeDtypeStruct((2, 2, channels), jnp.float32),
-        ),
-        in_specs=[hbm] * 9,
-        out_specs=(hbm,) * 6,
-        scratch_shapes=[
             pltpu.VMEM((held, channels), jnp.bfloat16),
             pltpu.VMEM((2, 6 * channels, channels), jnp.float32),
             pltpu.VMEM((2, 4 * channels), jnp.float32),
             pltpu.VMEM((2, 2, channels), jnp.float32),
             pltpu.VMEM((2, 2, channels), jnp.float32),
             pltpu.VMEM((2, 2, channels), jnp.float32),
+        ),
+        in_specs=[hbm] * 9,
+        out_specs=(vmem,) * 6,
+        scratch_shapes=[
             pltpu.VMEM(proj_weight.shape, jnp.bfloat16),
             pltpu.VMEM(gate_weight.shape, jnp.bfloat16),
             pltpu.VMEM(out_weight.shape, jnp.bfloat16),
@@ -721,7 +695,6 @@
             half_rows,
             pltpu.VMEM((dp, 2, 10, channels), jnp.float32),
             pltpu.SemaphoreType.DMA((9,)),
-            pltpu.SemaphoreType.DMA((8,)),
             pltpu.SemaphoreType.DMA((2, dap - 1)),
             pltpu.SemaphoreType.DMA((2, dap - 1)),
             pltpu.SemaphoreType.DMA((3,)),
@@ -734,7 +707,7 @@
             pltpu.SemaphoreType.DMA((dp - 1,)),
         ],
         compiler_params=pltpu.CompilerParams(
-            collective_id=0, has_side_effects=True, vmem_limit_bytes=62 * 1024 * 1024
+            collective_id=0, has_side_effects=True, vmem_limit_bytes=60 * 1024 * 1024
         ),
         name="triangle_updates",
     )(
@@ -760,10 +733,9 @@
             jax.ShapeDtypeStruct((2, 2, channels), jnp.float32),
             jax.ShapeDtypeStruct((2, 2, channels), jnp.float32),
         ),
-        in_specs=[hbm] * 6,
+        in_specs=[vmem] * 6,
         out_specs=(hbm,) * 8,
         scratch_shapes=[pltpu.SemaphoreType.DMA((8,))],
-        compiler_params=pltpu.CompilerParams(vmem_limit_bytes=62 * 1024 * 1024),
         name="deliver",
     )(*summed)
     return (outputs[0].T.reshape(1, channels, rows, width),) + tuple(outputs[1:])

time: 47.6 us -> 27.5 us (0.58)
  Pallas kernels: 46.8 us -> 22.9 us
  local copies, waits for them, and re-layouts: 0 us -> 3.76 us
    pallas_call x1, Pallas kernels: 25.8 us -> 2.09 us  [fused_body(): pl.pallas_call(deliver_kernel, out_shape=(jax.ShapeDtypeStruct((held, cha...]
    unnamed x0 -> x12, local copies, waits for them, and re-layouts: none -> 3.76 us
where the time goes in v3:
time: 27.5 us; the launch traced here: 27.3 us
  Pallas kernels  22.9 us (83%)
  local copies, waits for them, and re-layouts  3.76 us (14%)
  between operations  0.66 us (2%)
    pallas_call x1, Pallas kernels, fused_body(): pl.pallas_call(functools.partial(fused_kernel, peers, width), out_shape=(...  20.8 us
    unnamed x12, local copies, waits for them, and re-layouts  3.76 us
    pallas_call x1, Pallas kernels, fused_body(): pl.pallas_call(deliver_kernel, out_shape=(jax.ShapeDtypeStruct((held, cha...  2.09 us

profile of v3, /device:TPU:0, one launch (start us, length us, event | category | flops | bytes accessed | tf_op | source)
XLA Modules:
  0.0 27.3 jit_solution(7900610563328054753)
XLA Ops:
  0.6 20.8 %triangle_updates.1 = (bf16[64,128]{1,0:T(8,128)(2,1)S(1)}, f32[2,768,128]{2,1,0:T(8,128)S(1)}, f32[2,512]{1,0:T(2,128)S(1)}, f32[2,2,128]{2,1,0:T(2,128)S(1)}, ...) custom-call(bf16[64,128]{1,0:T(8,128)(2,1)} %bitcast.9, bf16[64,128]{1,0:T(8,128)(2,1)} %bitcast.10, ...), custom_call_target="tpu_custom_call" | custom-call | tf_op jit(solution)/shard_map/triangle_updates/pallas_call | solution.py:663
  21.4 0.0 copy-start
  21.4 0.9 %copy-done = f32[2,768,128]{2,1,0:T(8,128)} copy-done((f32[2,768,128]{2,1,0:T(8,128)}, f32[2,768,128]{2,1,0:T(8,128)S(1)}, u32[]{:S(2)}) %copy-start) | copy-done | bytes 786456
  22.3 0.0 copy-start.1
  22.3 0.6 %copy-done.1 = bf16[64,128]{1,0:T(8,128)(2,1)} copy-done((bf16[64,128]{1,0:T(8,128)(2,1)}, bf16[64,128]{1,0:T(8,128)(2,1)S(1)}, u32[]{:S(2)}) %copy-start.1) | copy-done | bytes 16408
  22.9 0.0 copy-start.3
  22.9 0.6 %copy-done.3 = f32[2,2,128]{2,1,0:T(2,128)} copy-done((f32[2,2,128]{2,1,0:T(2,128)}, f32[2,2,128]{2,1,0:T(2,128)S(1)}, u32[]{:S(2)}) %copy-start.3) | copy-done | bytes 2072
  23.5 0.0 copy-start.4
  23.5 0.6 %copy-done.4 = f32[2,2,128]{2,1,0:T(2,128)} copy-done((f32[2,2,128]{2,1,0:T(2,128)}, f32[2,2,128]{2,1,0:T(2,128)S(1)}, u32[]{:S(2)}) %copy-start.4) | copy-done | bytes 2072
  24.0 0.0 copy-start.5
  24.1 0.6 %copy-done.5 = f32[2,2,128]{2,1,0:T(2,128)} copy-done((f32[2,2,128]{2,1,0:T(2,128)}, f32[2,2,128]{2,1,0:T(2,128)S(1)}, u32[]{:S(2)}) %copy-start.5) | copy-done | bytes 2072
  24.6 0.0 copy-start.2
  24.6 0.6 %copy-done.2 = f32[2,512]{1,0:T(2,128)} copy-done((f32[2,512]{1,0:T(2,128)}, f32[2,512]{1,0:T(2,128)S(1)}, u32[]{:S(2)}) %copy-start.2) | copy-done | bytes 4120
  25.2 2.1 %deliver.1 = (bf16[64,128]{1,0:T(8,128)(2,1)}, f32[2,512,128]{2,1,0:T(8,128)}, f32[2,512]{1,0:T(2,128)}, f32[2,128,128]{2,1,0:T(8,128)}, f32[2,128,128]{2,1,0:T(...) custom-call(bf16[64,128]{1,0:T(8,128)(2,1)} %copy-done.1, f32[2,768,128]{2,1,0:T(8,128)} %copy-done, ...), custom_call_target="tpu_custom_call" | custom-call | tf_op jit(solution)/shard_map/deliver/pallas_call | solution.py:724
Async XLA Ops:
  21.4 0.9 %copy-start = (f32[2,768,128]{2,1,0:T(8,128)}, f32[2,768,128]{2,1,0:T(8,128)S(1)}, u32[]{:S(2)}) copy-start(f32[2,768,128]{2,1,0:T(8,128)S(1)} %get-tuple-element.23.big_ref) | copy-start | bytes 2359300
  22.3 0.6 %copy-start.1 = (bf16[64,128]{1,0:T(8,128)(2,1)}, bf16[64,128]{1,0:T(8,128)(2,1)S(1)}, u32[]{:S(2)}) copy-start(bf16[64,128]{1,0:T(8,128)(2,1)S(1)} %get-tuple-element.22.dpair_ref) | copy-start | bytes 49156
  22.9 0.6 %copy-start.3 = (f32[2,2,128]{2,1,0:T(2,128)}, f32[2,2,128]{2,1,0:T(2,128)S(1)}, u32[]{:S(2)}) copy-start(f32[2,2,128]{2,1,0:T(2,128)S(1)} %get-tuple-element.25.dchan_ref) | copy-start | bytes 6148
  23.5 0.6 %copy-start.4 = (f32[2,2,128]{2,1,0:T(2,128)}, f32[2,2,128]{2,1,0:T(2,128)S(1)}, u32[]{:S(2)}) copy-start(f32[2,2,128]{2,1,0:T(2,128)S(1)} %get-tuple-element.26.dgain_ref) | copy-start | bytes 6148
  24.0 0.6 %copy-start.5 = (f32[2,2,128]{2,1,0:T(2,128)}, f32[2,2,128]{2,1,0:T(2,128)S(1)}, u32[]{:S(2)}) copy-start(f32[2,2,128]{2,1,0:T(2,128)S(1)} %get-tuple-element.27.dshift_ref) | copy-start | bytes 6148
  24.6 0.6 %copy-start.2 = (f32[2,512]{1,0:T(2,128)}, f32[2,512]{1,0:T(2,128)S(1)}, u32[]{:S(2)}) copy-start(f32[2,512]{1,0:T(2,128)S(1)} %get-tuple-element.24.dbias_ref) | copy-start | bytes 12292

commit v4 on v3

--- a/solution.py
+++ b/solution.py
@@ -280,10 +280,11 @@
             row = a_ref[pl.ds(m * width + p if a_turned else p * width + m, 1), :]
             term = row * blocks[m]
             total = term if total is None else total + term
-        o_ref[pl.ds(pl.multiple_of(p * width, width), width), :] = total
+        o_ref[pl.ds(p * width, width), :] = total
         return carry
 
-    lax.fori_loop(0, width, step, 0)
+    for p in range(width):
+        step(p, 0)
 
 
 def fused_kernel(
@@ -477,6 +478,8 @@
             grad_inputs = grad_inputs + jnp.dot(
                 part, proj_ref[layer, lines, :], preferred_element_type=jnp.float32
             )
+            if index % 2 == 1 and layer == 0:
+                exchange_half(2 + index // 2)
         put_small(layer, 6, column_sum(grad_inputs * standard_in))
         put_small(layer, 8, column_sum(grad_inputs))
         return upstream + norm_lanes_back(
@@ -486,7 +489,8 @@
     pieces = (
         (1, 0, 6 * channels),
         (0, 4 * channels, 2 * channels),
-        (0, 0, 4 * channels),
+        (0, 0, 2 * channels),
+        (0, 2 * channels, 2 * channels),
     )
     flights = {}
 
@@ -562,8 +566,8 @@
     grad_logit = backward_near(grad_middle, saved_first, 0)
     exchange_half(1)
     exchange_sum(0)
+    exchange_sum(1)
     grad_start = backward_far(grad_middle, saved_first, grad_logit, 0)
-    exchange_half(2)
     small_all[at] = rows_s[...]
     small_copies = []
     for k in range(1, dp):
@@ -577,8 +581,8 @@
         )
         copy.start()
         small_copies.append(copy)
-    exchange_sum(1)
     exchange_sum(2)
+    exchange_sum(3)
     dleft_s[...] = grad_start
     dpair_ref[...] = dleft_s[own, :].astype(jnp.bfloat16)
     share(0)
@@ -594,9 +598,10 @@
     dgain_ref[...] = total[:, 6:8]
     dshift_ref[...] = total[:, 8:10]
     share(2)
-    for index in range(3):
+    share(3)
+    for index in range(4):
         flights[index][2].wait_recv()
-    for index in range(3):
+    for index in range(4):
         for copy in flights[index]:
             copy.wait_send()
     for copy in gathers[0] + gathers[1] + small_copies:
@@ -697,12 +702,12 @@
             pltpu.SemaphoreType.DMA((9,)),
             pltpu.SemaphoreType.DMA((2, dap - 1)),
             pltpu.SemaphoreType.DMA((2, dap - 1)),
-            pltpu.SemaphoreType.DMA((3,)),
-            pltpu.SemaphoreType.DMA((3,)),
-            pltpu.SemaphoreType.DMA((3,)),
-            pltpu.SemaphoreType.DMA((3,)),
-            pltpu.SemaphoreType.DMA((3,)),
-            pltpu.SemaphoreType.DMA((3,)),
+            pltpu.SemaphoreType.DMA((4,)),
+            pltpu.SemaphoreType.DMA((4,)),
+            pltpu.SemaphoreType.DMA((4,)),
+            pltpu.SemaphoreType.DMA((4,)),
+            pltpu.SemaphoreType.DMA((4,)),
+            pltpu.SemaphoreType.DMA((4,)),
             pltpu.SemaphoreType.DMA((dp - 1,)),
             pltpu.SemaphoreType.DMA((dp - 1,)),
         ],
@@ -736,6 +741,7 @@
         in_specs=[vmem] * 6,
         out_specs=(hbm,) * 8,
         scratch_shapes=[pltpu.SemaphoreType.DMA((8,))],
+        compiler_params=pltpu.CompilerParams(vmem_limit_bytes=4 * 1024 * 1024),
         name="deliver",
     )(*summed)
     return (outputs[0].T.reshape(1, channels, rows, width),) + tuple(outputs[1:])

time: 27.5 us -> 21.6 us (0.79)
  local copies, waits for them, and re-layouts: 3.76 us -> 0 us
  Pallas kernels: 22.9 us -> 20.8 us
    unnamed x12 -> x0, local copies, waits for them, and re-layouts: 3.76 us -> none
    pallas_call x1, Pallas kernels: 2.09 us -> 0.95 us  [fused_body(): pl.pallas_call(deliver_kernel, out_shape=(jax.ShapeDtypeStruct((held, cha...]
    pallas_call x1, Pallas kernels: 20.8 us -> 19.8 us  [fused_body(): pl.pallas_call(functools.partial(fused_kernel, peers, width), out_shape=(...]
where the time goes in v4:
time: 21.6 us; the launch traced here: 21.4 us
  Pallas kernels  20.8 us (96%)
  between operations  0.64 us (3%)
    pallas_call x1, Pallas kernels, fused_body(): pl.pallas_call(functools.partial(fused_kernel, peers, width), out_shape=(...  19.8 us
    pallas_call x1, Pallas kernels, fused_body(): pl.pallas_call(deliver_kernel, out_shape=(jax.ShapeDtypeStruct((held, cha...  0.95 us

profile of v4, /device:TPU:0, one launch (start us, length us, event | category | flops | bytes accessed | tf_op | source)
XLA Modules:
  0.0 21.4 jit_solution(11323157403964110394)
XLA Ops:
  0.6 19.8 %triangle_updates.1 = (bf16[64,128]{1,0:T(8,128)(2,1)S(1)}, f32[2,768,128]{2,1,0:T(8,128)S(1)}, f32[2,512]{1,0:T(2,128)S(1)}, f32[2,2,128]{2,1,0:T(2,128)S(1)}, ...) custom-call(bf16[64,128]{1,0:T(8,128)(2,1)} %bitcast.9, bf16[64,128]{1,0:T(8,128)(2,1)} %bitcast.10, ...), custom_call_target="tpu_custom_call" | custom-call | tf_op jit(solution)/shard_map/triangle_updates/pallas_call | solution.py:668
  20.5 1.0 %deliver.1 = (bf16[64,128]{1,0:T(8,128)(2,1)}, f32[2,512,128]{2,1,0:T(8,128)}, f32[2,512]{1,0:T(2,128)}, f32[2,128,128]{2,1,0:T(8,128)}, f32[2,128,128]{2,1,0:T(...) custom-call(bf16[64,128]{1,0:T(8,128)(2,1)S(1)} %get-tuple-element.22.dpair_ref, ...), custom_call_target="tpu_custom_call" | custom-call | tf_op jit(solution)/shard_map/deliver/pallas_call | solution.py:729

commit v5 on v4

--- a/solution.py
+++ b/solution.py
@@ -478,6 +478,8 @@
             grad_inputs = grad_inputs + jnp.dot(
                 part, proj_ref[layer, lines, :], preferred_element_type=jnp.float32
             )
+            if index == 0 and layer == 0:
+                exchange_sum(1)
             if index % 2 == 1 and layer == 0:
                 exchange_half(2 + index // 2)
         put_small(layer, 6, column_sum(grad_inputs * standard_in))
@@ -566,7 +568,6 @@
     grad_logit = backward_near(grad_middle, saved_first, 0)
     exchange_half(1)
     exchange_sum(0)
-    exchange_sum(1)
     grad_start = backward_far(grad_middle, saved_first, grad_logit, 0)
     small_all[at] = rows_s[...]
     small_copies = []

time: 21.6 us -> 21.6 us (level)
  no operation moved by 1% of the time
where the time goes in v5:
time: 21.6 us; the launch traced here: 21.4 us
  Pallas kernels  20.8 us (96%)
  between operations  0.64 us (3%)
    pallas_call x1, Pallas kernels, fused_body(): pl.pallas_call(functools.partial(fused_kernel, peers, width), out_shape=(...  19.8 us
    pallas_call x1, Pallas kernels, fused_body(): pl.pallas_call(deliver_kernel, out_shape=(jax.ShapeDtypeStruct((held, cha...  0.95 us

profile of v5, /device:TPU:0, one launch (start us, length us, event | category | flops | bytes accessed | tf_op | source)
XLA Modules:
  0.0 21.4 jit_solution(10209503756139207430)
XLA Ops:
  0.6 19.8 %triangle_updates.1 = (bf16[64,128]{1,0:T(8,128)(2,1)S(1)}, f32[2,768,128]{2,1,0:T(8,128)S(1)}, f32[2,512]{1,0:T(2,128)S(1)}, f32[2,2,128]{2,1,0:T(2,128)S(1)}, ...) custom-call(bf16[64,128]{1,0:T(8,128)(2,1)} %bitcast.9, bf16[64,128]{1,0:T(8,128)(2,1)} %bitcast.10, ...), custom_call_target="tpu_custom_call" | custom-call | tf_op jit(solution)/shard_map/triangle_updates/pallas_call | solution.py:669
  20.5 1.0 %deliver.1 = (bf16[64,128]{1,0:T(8,128)(2,1)}, f32[2,512,128]{2,1,0:T(8,128)}, f32[2,512]{1,0:T(2,128)}, f32[2,128,128]{2,1,0:T(8,128)}, f32[2,128,128]{2,1,0:T(...) custom-call(bf16[64,128]{1,0:T(8,128)(2,1)S(1)} %get-tuple-element.22.dpair_ref, ...), custom_call_target="tpu_custom_call" | custom-call | tf_op jit(solution)/shard_map/deliver/pallas_call | solution.py:730
